TPU v7x, 32 devices: a whole 2x2x4 slice. The times are simulated.
32 devices in a mesh: slab: 2 (over x), plane: 8 (over z, y), brick: 2 (over core).
Axes of the slice: x: 2, y: 2, z: 4, core: 2. Of those that a mesh axis runs over, the one named last changes fastest.
Arguments:
- camera_rows: bfloat16 [4, 16, 32, 2048], P(None, 'slab', ('plane', 'brick')), parts along dimension 1, may hold values from 0.19921875 to 5
- estimate: float32 [16, 32, 2048], P('slab', None, ('plane', 'brick')), parts along dimension 0, may hold values from 0.2 to 5
- psf_bank: float32 [32, 4, 3, 31], P(('slab', 'plane', 'brick')), parts along dimension 0, may hold values from 0 to 1.25, as said below
- psf_owner: int32 [32], P('slab'), parts along dimension 0, may hold values from 0 to 15, each once
- view_mask: int32 [32, 4], P('slab'), parts along dimension 0, may hold values 0 or 1
Outputs:
- deconvolved: float32 [16, 32, 2048], P('slab', None, ('plane', 'brick')), parts along dimension 0
There are 2 independent parts, one for each index of `slab`. A program takes and returns all parts, laid end to end along the dimension named above; each array names one. Nothing has to cross between parts.
Inputs may be any that keep to these rules, and one draw needn't show every extreme that they name: `psf_owner`: every brick names a different device: the map is a permutation of 0 to 15. `psf_bank`: every tap is positive.
All inputs are finite; a program needn't handle non-finite values.
Results may differ from a plain program's by a relative error of at most 0.0003.
Values may be sent and summed in bfloat16 or wider, within the bound.
A program may use at most 192 MiB of HBM per device.

v0:
```python
import jax
import jax.numpy as jnp
from jax import lax
from jax.sharding import PartitionSpec as P

V = 4
RADIUS = 15
ITERS = 2
BACKGROUND = 0.1
HIGHEST = lax.Precision.HIGHEST


def padded_2(cells, sides, width):
    for axis, dim in sides:
        count = lax.axis_size(axis)
        ends = count - 1
        head = lax.slice_in_dim(cells, 0, width, axis=dim)
        tail = lax.slice_in_dim(cells, cells.shape[dim] - width, cells.shape[dim], axis=dim)
        cells = jnp.concatenate(
            [
                lax.ppermute(tail, axis, [(i, (i + 1) % count) for i in range(ends)]),
                cells,
                lax.ppermute(head, axis, [((i + 1) % count, i) for i in range(ends)]),
            ],
            axis=dim,
        )
    return cells


def banded(profiles, size_in, size_out, offset):
    tap_count = profiles.shape[-1]
    centre = tap_count // 2
    lag_index = (
        jnp.arange(size_in, dtype=jnp.int32)[:, None]
        - jnp.arange(size_out, dtype=jnp.int32)[None, :]
        - offset
        + centre
    )
    one_hot = (
        lag_index[:, :, None] == jnp.arange(tap_count, dtype=jnp.int32)[None, None, :]
    ).astype(jnp.float32)
    return jnp.einsum("ijt,vt->vij", one_hot, profiles, precision=HIGHEST)


def across_columns(volume, band_x):
    if volume.ndim == 3:
        return jnp.einsum("zyi,vij->vzyj", volume, band_x, precision=HIGHEST)
    return jnp.einsum("vzyi,vij->vzyj", volume, band_x, precision=HIGHEST)


def across_rows(volume, band_y):
    view_count, depth_count, row_count, col_count = volume.shape
    block_rows = band_y.shape[2]
    margin = (band_y.shape[1] - block_rows) // 2
    pieces = volume.reshape(view_count, depth_count, row_count // block_rows, block_rows, col_count)
    blanks = jnp.zeros((view_count, depth_count, 1, margin, col_count), jnp.float32)
    before = jnp.concatenate([blanks, pieces[:, :, :-1, block_rows - margin :, :]], axis=2)
    behind = jnp.concatenate([pieces[:, :, 1:, :margin, :], blanks], axis=2)
    windows = jnp.concatenate([before, pieces, behind], axis=3)
    result = jnp.einsum("vzqic,vij->vzqjc", windows, band_y, precision=HIGHEST)
    return result.reshape(view_count, depth_count, row_count, col_count)


def across_depth(volume, band_z):
    return jnp.einsum("vzyc,vzw->vwyc", volume, band_z, precision=HIGHEST)


def separable(volume, bands):
    return across_depth(across_rows(across_columns(volume, bands[0]), bands[1]), bands[2])


def shards(camera_rows, estimate, psf_bank, psf_owner, view_mask):
    regrouped = lax.all_to_all(
        camera_rows, ("plane", "brick"), split_axis=3, concat_axis=2, tiled=True
    )
    position = lax.axis_index(("plane", "brick"))
    brick_ids = jnp.arange(psf_owner.shape[0], dtype=jnp.int32)
    is_mine = brick_ids == position
    owner_id = jnp.sum(jnp.where(is_mine, psf_owner, 0))
    observed = jnp.sum(jnp.where(is_mine[:, None], view_mask, 0), axis=0) > 0
    fitted = lax.all_gather(psf_bank, ("plane", "brick"), axis=0, tiled=True)
    chosen = (brick_ids == owner_id).astype(jnp.float32)
    kernels = jnp.einsum("b,bvat->vat", chosen, fitted, precision=HIGHEST)
    kernels = kernels / jnp.sum(kernels, axis=-1, keepdims=True)
    flipped = kernels[:, :, ::-1]
    depth_size = estimate.shape[0]
    row_size = estimate.shape[1]
    col_size = estimate.shape[2]
    block_size = 128 if row_size % 128 == 0 else row_size

    def make_bands(profiles):
        return (
            banded(profiles[:, 2], col_size + 2 * RADIUS, col_size, RADIUS),
            banded(profiles[:, 1], block_size + 2 * RADIUS, block_size, RADIUS),
            banded(profiles[:, 0], depth_size, depth_size, 0),
        )

    blur_bands = make_bands(kernels)
    back_bands = make_bands(flipped)
    current = estimate
    for iteration in range(ITERS):
        padded = padded_2(current.astype(jnp.bfloat16), ((("plane", "brick"), 2),), RADIUS).astype(
            current.dtype
        )
        blurred = separable(padded, blur_bands)
        quotient = jnp.where(
            observed[:, None, None, None],
            regrouped.astype(jnp.float32) / (blurred + BACKGROUND),
            0.0,
        )
        quotient_wide = padded_2(
            quotient.astype(jnp.bfloat16), ((("plane", "brick"), 3),), RADIUS
        ).astype(quotient.dtype)
        corrected = separable(quotient_wide, back_bands)
        factor = jnp.sum(jnp.where(observed[:, None, None, None], corrected, 1.0), axis=0) / V
        current = current * factor
    return current


def solution(mesh):
    return jax.shard_map(
        shards,
        mesh=mesh,
        in_specs=(
            P(None, "slab", ("plane", "brick"), None),
            P("slab", None, ("plane", "brick")),
            P(("slab", "plane", "brick"), None, None, None),
            P("slab"),
            P("slab", None),
        ),
        out_specs=P("slab", None, ("plane", "brick")),
        check_vma=False,
    )
```

profile of v0, /device:TPU:1, one launch (start us, length us, event | category | flops | bytes accessed | tf_op | source)
XLA Modules:
  0.0 100.3 jit_solution(6253015987272240798)
XLA Ops:
  0.0 6.3 %copy.47 = bf16[4,8,2,2048]{1,0,2,3:T(4,128)(2,1)} copy(bf16[4,8,2,2048]{3,2,1,0:T(2,128)(2,1)} %param.5) | data formatting | bytes 524288 | tf_op args[0]
  6.4 6.5 %reshape.127 = bf16[16,2,4096]{2,1,0:T(2,128)(2,1)} reshape(bf16[2048,2,4,8]{3,2,1,0:T(4,128)(2,1)} %bitcast.116) | data formatting | bytes 524288
  12.8 7.3 %all-to-all-start = ((bf16[16,2,4096]{2,1,0:T(2,128)(2,1)}), bf16[16,2,4096]{2,1,0:T(2,128)(2,1)S(1)}, u32[]{:S(2)}, u32[]{:S(2)}) async-start(bf16[16,2,4096]{2,1,0:T(2,128)(2,1)} %reshape.127), calls=%async_computation | async-start | bytes 524288 | tf_op jit(solution)/shard_map/all_to_all | solution.py:73
  20.3 2.0 %collective-permute-start.1 = (bf16[8,32,15]{2,1,0:T(8,128)(2,1)S(1)}, bf16[8,32,15]{2,1,0:T(8,128)(2,1)S(1)}, u32[]{:S(2)}, u32[]{:S(2)}) collective-permute-start(bf16[8,32,15]{2,1,0:T(8,128)(2,1)S(1)} %get-tuple-element.12), channel_id=1, source_target_pairs={{1,0},{2,1},{3,2},{4,3},{5,4},{6,5},{7,6},{8,7},{9,8},{10,9},{11,1... | collective-permute-start | bytes 23048 | tf_op jit(solution)/shard_map/ppermute | solution.py:23
  22.3 3.5 %collective-permute-start = (bf16[8,32,15]{2,1,0:T(8,128)(2,1)S(1)}, bf16[8,32,15]{2,1,0:T(8,128)(2,1)S(1)}, u32[]{:S(2)}, u32[]{:S(2)}) collective-permute-start(bf16[8,32,15]{2,1,0:T(8,128)(2,1)S(1)} %get-tuple-element.11), channel_id=1, source_target_pairs={{0,1},{1,2},{2,3},{3,4},{4,5},{5,6},{6,7},{7,8},{8,9},{9,10},{10,1... | collective-permute-start | bytes 23048 | tf_op jit(solution)/shard_map/ppermute | solution.py:21
  25.9 20.7 %all_gather.3 = f32[16,4,3,31]{3,1,2,0:T(4,128)S(1)} all-gather(f32[1,4,3,31]{3,1,2,0:T(4,128)S(1)} %copy-done.1), channel_id=1, replica_groups=mesh['slab'=2,'plane'=8,'brick'=2] {'plane','brick'}, dimensions={0}, use_global_device_ids=true | all-gather | bytes 25296 | tf_op jit(solution)/shard_map/all_gather | solution.py:81
  46.6 0.6 select_reduce_fusion.1
  47.2 0.8 fusion.48
  48.2 0.9 fusion.12
  49.1 0.3 convolution_bitcast_fusion.8
  49.4 0.1 select_reduce_fusion
  49.5 0.1 slice.54
  49.6 0.9 fusion.13
  50.5 0.1 slice.48
  50.6 0.3 convolution_bitcast_fusion.9
  50.9 0.4 convolution_bitcast_fusion.10
  51.3 0.1 slice.46
  51.5 0.5 convolution_bitcast_fusion.1
  52.0 0.7 convolution_bitcast_fusion.7
  52.7 5.9 %reshape.128 = bf16[2048,2,4,8]{3,2,1,0:T(4,128)(2,1)} reshape(bf16[16,2,4096]{2,1,0:T(2,128)(2,1)S(1)} %all-to-all-done) | data formatting | bytes 524288
  58.7 5.9 %copy.48 = f32[4,8,2,16,128]{4,1,2,3,0:T(8,128)S(1)} copy(bf16[4,8,2,16,128]{1,0,2,4,3:T(4,128)(2,1)} %bitcast.115) | data formatting | bytes 786432 | tf_op jit(solution)/shard_map/convert_element_type | solution.py:108
  64.6 0.9 fusion.8
  65.5 0.1 fusion.77
  65.6 2.1 %collective-permute-start.3 = (bf16[4,8,32,15]{3,1,2,0:T(8,128)(2,1)S(1)}, bf16[4,8,32,15]{3,1,2,0:T(8,128)(2,1)S(1)}, u32[]{:S(2)}, u32[]{:S(2)}) collective-permute-start(bf16[4,8,32,15]{3,1,2,0:T(8,128)(2,1)S(1)} %get-tuple-element.8), channel_id=1, source_target_pairs={{1,0},{2,1},{3,2},{4,3},{5,4},{6,5},{7,6},{8,7},{9,8},{10,9},{11,1... | collective-permute-start | bytes 92168 | tf_op jit(solution)/shard_map/ppermute | solution.py:23
  67.7 3.5 %collective-permute-start.2 = (bf16[4,8,32,15]{3,1,2,0:T(8,128)(2,1)S(1)}, bf16[4,8,32,15]{3,1,2,0:T(8,128)(2,1)S(1)}, u32[]{:S(2)}, u32[]{:S(2)}) collective-permute-start(bf16[4,8,32,15]{3,1,2,0:T(8,128)(2,1)S(1)} %get-tuple-element.7), channel_id=1, source_target_pairs={{0,1},{1,2},{2,3},{3,4},{4,5},{5,6},{6,7},{7,8},{8,9},{9,10},{10,1... | collective-permute-start | bytes 92168 | tf_op jit(solution)/shard_map/ppermute | solution.py:21
  71.2 0.4 convolution_bitcast_fusion.11
  71.7 1.6 %collective-permute-done.3 = bf16[4,8,32,15]{3,1,2,0:T(8,128)(2,1)S(1)} collective-permute-done((bf16[4,8,32,15]{3,1,2,0:T(8,128)(2,1)S(1)}, bf16[4,8,32,15]{3,1,2,0:T(8,128)(2,1)S(1)}, u32[]{:S(2)}, u32[]{:S(2)}) %collective-permute-start.3) | collective-permute-done | bytes 30752 | tf_op jit(solution)/shard_map/ppermute | solution.py:23
  73.3 1.2 %collective-permute-done.2 = bf16[4,8,32,15]{3,1,2,0:T(8,128)(2,1)S(1)} collective-permute-done((bf16[4,8,32,15]{3,1,2,0:T(8,128)(2,1)S(1)}, bf16[4,8,32,15]{3,1,2,0:T(8,128)(2,1)S(1)}, u32[]{:S(2)}, u32[]{:S(2)}) %collective-permute-start.2) | collective-permute-done | bytes 30752 | tf_op jit(solution)/shard_map/ppermute | solution.py:21
  74.5 0.3 pad_maximum_fusion.8
  74.8 0.6 convolution_bitcast_fusion.6
  75.4 0.7 convolution_bitcast_fusion.5
  76.1 0.8 fusion.10
  77.1 1.9 %collective-permute-start.5 = (bf16[8,32,15]{2,1,0:T(8,128)(2,1)S(1)}, bf16[8,32,15]{2,1,0:T(8,128)(2,1)S(1)}, u32[]{:S(2)}, u32[]{:S(2)}) collective-permute-start(bf16[8,32,15]{2,1,0:T(8,128)(2,1)S(1)} %get-tuple-element.10), channel_id=1, source_target_pairs={{1,0},{2,1},{3,2},{4,3},{5,4},{6,5},{7,6},{8,7},{9,8},{10,9},{11,1... | collective-permute-start | bytes 23048 | tf_op jit(solution)/shard_map/ppermute | solution.py:23
  79.0 4.6 %collective-permute-start.4 = (bf16[8,32,15]{2,1,0:T(8,128)(2,1)S(1)}, bf16[8,32,15]{2,1,0:T(8,128)(2,1)S(1)}, u32[]{:S(2)}, u32[]{:S(2)}) collective-permute-start(bf16[8,32,15]{2,1,0:T(8,128)(2,1)S(1)} %get-tuple-element.9), channel_id=1, source_target_pairs={{0,1},{1,2},{2,3},{3,4},{4,5},{5,6},{6,7},{7,8},{8,9},{9,10},{10,1... | collective-permute-start | bytes 23048 | tf_op jit(solution)/shard_map/ppermute | solution.py:21
  83.6 1.1 %collective-permute-done.4 = bf16[8,32,15]{2,1,0:T(8,128)(2,1)S(1)} collective-permute-done((bf16[8,32,15]{2,1,0:T(8,128)(2,1)S(1)}, bf16[8,32,15]{2,1,0:T(8,128)(2,1)S(1)}, u32[]{:S(2)}, u32[]{:S(2)}) %collective-permute-start.4) | collective-permute-done | bytes 7712 | tf_op jit(solution)/shard_map/ppermute | solution.py:21
  84.7 0.4 convolution_bitcast_fusion
  85.2 0.7 convolution_bitcast_fusion.4
  85.9 0.9 fusion.9
  86.8 0.1 fusion.76
  86.9 1.9 %collective-permute-start.7 = (bf16[4,8,32,15]{3,1,2,0:T(8,128)(2,1)S(1)}, bf16[4,8,32,15]{3,1,2,0:T(8,128)(2,1)S(1)}, u32[]{:S(2)}, u32[]{:S(2)}) collective-permute-start(bf16[4,8,32,15]{3,1,2,0:T(8,128)(2,1)S(1)} %get-tuple-element.6), channel_id=1, source_target_pairs={{1,0},{2,1},{3,2},{4,3},{5,4},{6,5},{7,6},{8,7},{9,8},{10,9},{11,1... | collective-permute-start | bytes 92168 | tf_op jit(solution)/shard_map/ppermute | solution.py:23
  88.8 4.3 %collective-permute-start.6 = (bf16[4,8,32,15]{3,1,2,0:T(8,128)(2,1)S(1)}, bf16[4,8,32,15]{3,1,2,0:T(8,128)(2,1)S(1)}, u32[]{:S(2)}, u32[]{:S(2)}) collective-permute-start(bf16[4,8,32,15]{3,1,2,0:T(8,128)(2,1)S(1)} %get-tuple-element.5), channel_id=1, source_target_pairs={{0,1},{1,2},{2,3},{3,4},{4,5},{5,6},{6,7},{7,8},{8,9},{9,10},{10,1... | collective-permute-start | bytes 92168 | tf_op jit(solution)/shard_map/ppermute | solution.py:21
  93.1 2.1 %collective-permute-done.7 = bf16[4,8,32,15]{3,1,2,0:T(8,128)(2,1)S(1)} collective-permute-done((bf16[4,8,32,15]{3,1,2,0:T(8,128)(2,1)S(1)}, bf16[4,8,32,15]{3,1,2,0:T(8,128)(2,1)S(1)}, u32[]{:S(2)}, u32[]{:S(2)}) %collective-permute-start.7) | collective-permute-done | bytes 30752 | tf_op jit(solution)/shard_map/ppermute | solution.py:23
  95.2 1.9 %collective-permute-done.6 = bf16[4,8,32,15]{3,1,2,0:T(8,128)(2,1)S(1)} collective-permute-done((bf16[4,8,32,15]{3,1,2,0:T(8,128)(2,1)S(1)}, bf16[4,8,32,15]{3,1,2,0:T(8,128)(2,1)S(1)}, u32[]{:S(2)}, u32[]{:S(2)}) %collective-permute-start.6) | collective-permute-done | bytes 30752 | tf_op jit(solution)/shard_map/ppermute | solution.py:21
  97.1 0.3 pad_maximum_fusion.9
  97.5 0.6 convolution_bitcast_fusion.3
  98.0 0.7 convolution_bitcast_fusion.2
  98.8 0.8 fusion.11
  99.6 0.7 fusion.46
  (27 shorter events, 0.6 us)
Async XLA Ops:
  6.3 13.8 %copy-start = (f32[8,32,128]{2,1,0:T(8,128)S(1)}, f32[8,32,128]{2,1,0:T(8,128)}, u32[]{:S(2)}) copy-start(f32[8,32,128]{2,1,0:T(8,128)} %param.6) | copy-start | bytes 393220
  6.3 19.6 %copy-start.1 = (f32[1,4,3,31]{3,1,2,0:T(4,128)S(1)}, f32[1,4,3,31]{3,1,2,0:T(4,128)}, u32[]{:S(2)}) copy-start(f32[1,4,3,31]{3,1,2,0:T(4,128)} %param.7) | copy-start | bytes 4468
  6.3 40.3 %copy-start.3 = (s32[16]{0:T(128)S(1)}, s32[16]{0:T(128)}, u32[]{:S(2)}) copy-start(s32[16]{0:T(128)} %param.8) | copy-start | bytes 196
  6.3 43.1 %copy-start.2 = (s32[16,4]{0,1:T(4,128)S(1)}, s32[16,4]{0,1:T(4,128)}, u32[]{:S(2)}) copy-start(s32[16,4]{0,1:T(4,128)} %param.9) | copy-start | bytes 772
  12.8 39.9 %all-to-all-start = ((bf16[16,2,4096]{2,1,0:T(2,128)(2,1)}), bf16[16,2,4096]{2,1,0:T(2,128)(2,1)S(1)}, u32[]{:S(2)}, u32[]{:S(2)}) async-start(bf16[16,2,4096]{2,1,0:T(2,128)(2,1)} %reshape.127), calls=%async_computation | async-start | bytes 524288 | tf_op jit(solution)/shard_map/all_to_all | solution.py:73
  20.3 31.2 %collective-permute-start.1 = (bf16[8,32,15]{2,1,0:T(8,128)(2,1)S(1)}, bf16[8,32,15]{2,1,0:T(8,128)(2,1)S(1)}, u32[]{:S(2)}, u32[]{:S(2)}) collective-permute-start(bf16[8,32,15]{2,1,0:T(8,128)(2,1)S(1)} %get-tuple-element.12), channel_id=1, source_target_pairs={{1,0},{2,1},{3,2},{4,3},{5,4},{6,5},{7,6},{8,7},{9,8},{10,9},{11,1... | collective-permute-start | bytes 23048 | tf_op jit(solution)/shard_map/ppermute | solution.py:23
  22.3 29.2 %collective-permute-start = (bf16[8,32,15]{2,1,0:T(8,128)(2,1)S(1)}, bf16[8,32,15]{2,1,0:T(8,128)(2,1)S(1)}, u32[]{:S(2)}, u32[]{:S(2)}) collective-permute-start(bf16[8,32,15]{2,1,0:T(8,128)(2,1)S(1)} %get-tuple-element.11), channel_id=1, source_target_pairs={{0,1},{1,2},{2,3},{3,4},{4,5},{5,6},{6,7},{7,8},{8,9},{9,10},{10,1... | collective-permute-start | bytes 23048 | tf_op jit(solution)/shard_map/ppermute | solution.py:21
  65.6 7.7 %collective-permute-start.3 = (bf16[4,8,32,15]{3,1,2,0:T(8,128)(2,1)S(1)}, bf16[4,8,32,15]{3,1,2,0:T(8,128)(2,1)S(1)}, u32[]{:S(2)}, u32[]{:S(2)}) collective-permute-start(bf16[4,8,32,15]{3,1,2,0:T(8,128)(2,1)S(1)} %get-tuple-element.8), channel_id=1, source_target_pairs={{1,0},{2,1},{3,2},{4,3},{5,4},{6,5},{7,6},{8,7},{9,8},{10,9},{11,1... | collective-permute-start | bytes 92168 | tf_op jit(solution)/shard_map/ppermute | solution.py:23
  67.7 6.8 %collective-permute-start.2 = (bf16[4,8,32,15]{3,1,2,0:T(8,128)(2,1)S(1)}, bf16[4,8,32,15]{3,1,2,0:T(8,128)(2,1)S(1)}, u32[]{:S(2)}, u32[]{:S(2)}) collective-permute-start(bf16[4,8,32,15]{3,1,2,0:T(8,128)(2,1)S(1)} %get-tuple-element.7), channel_id=1, source_target_pairs={{0,1},{1,2},{2,3},{3,4},{4,5},{5,6},{6,7},{7,8},{8,9},{9,10},{10,1... | collective-permute-start | bytes 92168 | tf_op jit(solution)/shard_map/ppermute | solution.py:21
  77.1 6.5 %collective-permute-start.5 = (bf16[8,32,15]{2,1,0:T(8,128)(2,1)S(1)}, bf16[8,32,15]{2,1,0:T(8,128)(2,1)S(1)}, u32[]{:S(2)}, u32[]{:S(2)}) collective-permute-start(bf16[8,32,15]{2,1,0:T(8,128)(2,1)S(1)} %get-tuple-element.10), channel_id=1, source_target_pairs={{1,0},{2,1},{3,2},{4,3},{5,4},{6,5},{7,6},{8,7},{9,8},{10,9},{11,1... | collective-permute-start | bytes 23048 | tf_op jit(solution)/shard_map/ppermute | solution.py:23
  79.0 5.7 %collective-permute-start.4 = (bf16[8,32,15]{2,1,0:T(8,128)(2,1)S(1)}, bf16[8,32,15]{2,1,0:T(8,128)(2,1)S(1)}, u32[]{:S(2)}, u32[]{:S(2)}) collective-permute-start(bf16[8,32,15]{2,1,0:T(8,128)(2,1)S(1)} %get-tuple-element.9), channel_id=1, source_target_pairs={{0,1},{1,2},{2,3},{3,4},{4,5},{5,6},{6,7},{7,8},{8,9},{9,10},{10,1... | collective-permute-start | bytes 23048 | tf_op jit(solution)/shard_map/ppermute | solution.py:21
  86.9 8.3 %collective-permute-start.7 = (bf16[4,8,32,15]{3,1,2,0:T(8,128)(2,1)S(1)}, bf16[4,8,32,15]{3,1,2,0:T(8,128)(2,1)S(1)}, u32[]{:S(2)}, u32[]{:S(2)}) collective-permute-start(bf16[4,8,32,15]{3,1,2,0:T(8,128)(2,1)S(1)} %get-tuple-element.6), channel_id=1, source_target_pairs={{1,0},{2,1},{3,2},{4,3},{5,4},{6,5},{7,6},{8,7},{9,8},{10,9},{11,1... | collective-permute-start | bytes 92168 | tf_op jit(solution)/shard_map/ppermute | solution.py:23
  88.8 8.3 %collective-permute-start.6 = (bf16[4,8,32,15]{3,1,2,0:T(8,128)(2,1)S(1)}, bf16[4,8,32,15]{3,1,2,0:T(8,128)(2,1)S(1)}, u32[]{:S(2)}, u32[]{:S(2)}) collective-permute-start(bf16[4,8,32,15]{3,1,2,0:T(8,128)(2,1)S(1)} %get-tuple-element.5), channel_id=1, source_target_pairs={{0,1},{1,2},{2,3},{3,4},{4,5},{5,6},{6,7},{7,8},{8,9},{9,10},{10,1... | collective-permute-start | bytes 92168 | tf_op jit(solution)/shard_map/ppermute | solution.py:21
where the time goes:
time: 101 us; the launch traced here: 100 us
  starting transfers between devices  31.2 us (31%)
  local copies, waits for them, and re-layouts  25.6 us (25%)
  blocking collectives  20.7 us (20%)
  matrix products  12.2 us (12%)
  waiting for transfers between devices  7.98 us (8%)
  other arithmetic  2.37 us (2%)
    all_gather x1, blocking collectives, shards(): fitted = lax.all_gather(psf_bank, ('plane', 'brick'), axis=0, tiled=True)  20.7 us
    unnamed x11, local copies, waits for them, and re-layouts  18.8 us
    ppermute x4, starting transfers between devices, padded_2(): lax.ppermute(tail, axis, [(i, (i + 1) % count) for i in range(ends)])  15.9 us
    ppermute x4, starting transfers between devices, padded_2(): lax.ppermute(head, axis, [((i + 1) % count, i) for i in range(ends)])  7.93 us
    all_to_all x1, starting transfers between devices, shards(): lax.all_to_all(camera_rows, ('plane', 'brick'), split_axis=3, concat_axis...  7.35 us
    convert_element_type x1, local copies, waits for them, and re-layouts, shards(): regrouped.astype(jnp.float32) / (blurred + BACKGROUND)  5.93 us
    ppermute x4, waiting for transfers between devices, padded_2(): lax.ppermute(tail, axis, [(i, (i + 1) % count) for i in range(ends)])  4.22 us
    ppermute x4, waiting for transfers between devices, padded_2(): lax.ppermute(head, axis, [((i + 1) % count, i) for i in range(ends)])  3.76 us
  transfers between devices with their start and end apart: 9, of which 5 were waited for; matrix products, arithmetic and copies ran while one was open for 7% of the time, Pallas kernels for 0%

commit v1 on v0

--- a/solution.py
+++ b/solution.py
@@ -8,6 +8,13 @@
 ITERS = 2
 BACKGROUND = 0.1
 HIGHEST = lax.Precision.HIGHEST
+
+
+def stacked_exchange(value, mesh_axis, split, join):
+    n_dev = lax.axis_size(mesh_axis)
+    blocks = jnp.stack(jnp.split(value, n_dev, axis=split), axis=0)
+    blocks = lax.all_to_all(blocks, mesh_axis, split_axis=0, concat_axis=0)
+    return jnp.concatenate(blocks, axis=join)
 
 
 def padded_2(cells, sides, width):
@@ -70,9 +77,7 @@
 
 
 def shards(camera_rows, estimate, psf_bank, psf_owner, view_mask):
-    regrouped = lax.all_to_all(
-        camera_rows, ("plane", "brick"), split_axis=3, concat_axis=2, tiled=True
-    )
+    regrouped = stacked_exchange(camera_rows, ("plane", "brick"), 3, 2)
     position = lax.axis_index(("plane", "brick"))
     brick_ids = jnp.arange(psf_owner.shape[0], dtype=jnp.int32)
     is_mine = brick_ids == position

time: 101 us -> 90.2 us (0.89)
  local copies, waits for them, and re-layouts: 25.6 us -> 12.3 us
  waiting for transfers between devices: 7.98 us -> 13.2 us
  starting transfers between devices: 31.2 us -> 26.1 us
  blocking collectives: 20.7 us -> 21.9 us
  other arithmetic: 2.37 us -> 3.53 us
    ppermute x4, waiting for transfers between devices: 3.76 us -> 12.1 us  [padded_2(): lax.ppermute(head, axis, [((i + 1) % count, i) for i in range(ends)])]
    unnamed x11 -> x25, local copies, waits for them, and re-layouts: 18.8 us -> 10.7 us
    convert_element_type x1, local copies, waits for them, and re-layouts: 5.93 us -> 0.04 us  [shards(): regrouped.astype(jnp.float32) / (blurred + BACKGROUND)]
    ppermute x4, starting transfers between devices: 15.9 us -> 10.3 us  [padded_2(): lax.ppermute(tail, axis, [(i, (i + 1) % count) for i in range(ends)])]
    ppermute x4, waiting for transfers between devices: 4.22 us -> 1.09 us  [padded_2(): lax.ppermute(tail, axis, [(i, (i + 1) % count) for i in range(ends)])]
    ppermute x4, starting transfers between devices: 7.93 us -> 9.34 us  [padded_2(): lax.ppermute(head, axis, [((i + 1) % count, i) for i in range(ends)])]
    all_gather x1, blocking collectives: 20.7 us -> 21.9 us  [shards(): fitted = lax.all_gather(psf_bank, ('plane', 'brick'), axis=0, tiled=True)]
  transfers between devices with their start and end apart: 9 -> 9, of which waited for: 5 -> 5; matrix products, arithmetic and copies ran while one was open for 7% -> 20% of each run, Pallas kernels for 0% -> 0%
where the time goes in v1:
time: 90.2 us; the launch traced here: 89.5 us
  starting transfers between devices  26.1 us (29%)
  blocking collectives  21.9 us (24%)
  waiting for transfers between devices  13.2 us (15%)
  local copies, waits for them, and re-layouts  12.3 us (14%)
  matrix products  12.2 us (14%)
  other arithmetic  3.53 us (4%)
    all_gather x1, blocking collectives, shards(): fitted = lax.all_gather(psf_bank, ('plane', 'brick'), axis=0, tiled=True)  21.9 us
    ppermute x4, waiting for transfers between devices, padded_2(): lax.ppermute(head, axis, [((i + 1) % count, i) for i in range(ends)])  12.1 us
    unnamed x25, local copies, waits for them, and re-layouts  10.7 us
    ppermute x4, starting transfers between devices, padded_2(): lax.ppermute(tail, axis, [(i, (i + 1) % count) for i in range(ends)])  10.3 us
    ppermute x4, starting transfers between devices, padded_2(): lax.ppermute(head, axis, [((i + 1) % count, i) for i in range(ends)])  9.34 us
    all_to_all x1, starting transfers between devices, stacked_exchange(): blocks = lax.all_to_all(blocks, mesh_axis, split_axis=0, concat_axis=0)  6.45 us
    dot_general x4, matrix products, across_depth(): return jnp.einsum('vzyc,vzw->vwyc', volume, band_z, precision=HIGHEST)  3.35 us
    dot_general x6, matrix products, banded(): return jnp.einsum('ijt,vt->vij', one_hot, profiles, precision=HIGHEST)  3.14 us
  transfers between devices with their start and end apart: 9, of which 5 were waited for; matrix products, arithmetic and copies ran while one was open for 20% of the time, Pallas kernels for 0%

profile of v1, /device:TPU:1, one launch (start us, length us, event | category | flops | bytes accessed | tf_op | source)
XLA Modules:
  0.0 89.5 jit_solution(286209921248299283)
XLA Ops:
  0.0 1.0 %convert_element_type.36 = bf16[8,32,128]{2,1,0:T(8,128)(2,1)S(1)} convert(f32[8,32,128]{2,1,0:T(8,128)} %param.6) | non-fusion elementwise | flops 32768 | bytes 196608 | tf_op jit(solution)/shard_map/convert_element_type | solution.py:107
  1.1 4.5 %collective-permute-start = (bf16[8,32,15]{2,1,0:T(8,128)(2,1)S(1)}, bf16[8,32,15]{2,1,0:T(8,128)(2,1)S(1)}, u32[]{:S(2)}, u32[]{:S(2)}) collective-permute-start(bf16[8,32,15]{2,1,0:T(8,128)(2,1)S(1)} %get-tuple-element.11), channel_id=1, source_target_pairs={{0,1},{1,2},{2,3},{3,4},{4,5},{5,6},{6,7},{7,8},{8,9},{9,10},{10,1... | collective-permute-start | bytes 23048 | tf_op jit(solution)/shard_map/ppermute | solution.py:28
  5.6 1.9 %collective-permute-start.1 = (bf16[8,32,15]{2,1,0:T(8,128)(2,1)S(1)}, bf16[8,32,15]{2,1,0:T(8,128)(2,1)S(1)}, u32[]{:S(2)}, u32[]{:S(2)}) collective-permute-start(bf16[8,32,15]{2,1,0:T(8,128)(2,1)S(1)} %get-tuple-element.12), channel_id=1, source_target_pairs={{1,0},{2,1},{3,2},{4,3},{5,4},{6,5},{7,6},{8,7},{9,8},{10,9},{11,1... | collective-permute-start | bytes 23048 | tf_op jit(solution)/shard_map/ppermute | solution.py:30
  7.5 1.3 %constant_dynamic-update-slice_fusion.15 = bf16[16,4,8,2,128]{4,3,2,1,0:T(2,128)(2,1)} fusion(bf16[4,8,2,2048]{3,2,1,0:T(2,128)(2,1)} %param.5), kind=kLoop, calls=%fused_computation.100 | loop fusion | bytes 32768
  8.9 1.3 %constant_dynamic-update-slice_fusion.14 = bf16[16,4,8,2,128]{4,3,2,1,0:T(2,128)(2,1)} fusion(bf16[16,4,8,2,128]{4,3,2,1,0:T(2,128)(2,1)} %constant_dynamic-update-slice_fusion.15, bf16[4,8,2,2048]{3,2,1,0:T(2,128)(2,1)} %param.5), kind=kLoop, calls=%fused_computation.99 | loop fusion | bytes 32768
  10.2 0.6 constant_dynamic-update-slice_fusion.13
  10.8 0.6 constant_dynamic-update-slice_fusion.12
  11.4 0.6 constant_dynamic-update-slice_fusion.11
  12.0 0.6 constant_dynamic-update-slice_fusion.10
  12.7 0.6 constant_dynamic-update-slice_fusion.9
  13.3 0.6 constant_dynamic-update-slice_fusion.8
  13.9 0.6 constant_dynamic-update-slice_fusion.7
  14.5 0.6 constant_dynamic-update-slice_fusion.6
  15.1 0.6 constant_dynamic-update-slice_fusion.5
  15.7 0.6 constant_dynamic-update-slice_fusion.4
  16.3 0.6 constant_dynamic-update-slice_fusion.3
  16.9 0.6 constant_dynamic-update-slice_fusion.2
  17.6 0.6 constant_dynamic-update-slice_fusion.1
  18.2 0.6 constant_dynamic-update-slice_fusion
  18.8 6.5 %all-to-all-start = ((bf16[16,4,8,2,128]{4,3,2,1,0:T(2,128)(2,1)}), bf16[16,4,8,2,128]{4,3,2,1,0:T(2,128)(2,1)S(1)}, u32[]{:S(2)}, u32[]{:S(2)}) async-start(bf16[16,4,8,2,128]{4,3,2,1,0:T(2,128)(2,1)} %constant_dynamic-update-slice_fusion), calls=%async_computation | async-start | bytes 524288 | tf_op jit(solution)/shard_map/all_to_all | solution.py:16
  25.3 0.6 select_reduce_fusion.1
  25.9 21.9 %all_gather.3 = f32[16,4,3,31]{3,1,2,0:T(4,128)S(1)} all-gather(f32[1,4,3,31]{3,1,2,0:T(4,128)S(1)} %copy-done.2), channel_id=1, replica_groups=mesh['slab'=2,'plane'=8,'brick'=2] {'plane','brick'}, dimensions={0}, use_global_device_ids=true | all-gather | bytes 25296 | tf_op jit(solution)/shard_map/all_gather | solution.py:86
  47.8 0.8 fusion.48
  48.8 0.9 %fusion.12 = f32[4,158,128,1]{2,0,1,3:T(4,128)S(1)} fusion(s32[158,128]{1,0:T(8,128)S(1)} %iota_subtract_fusion, f32[4,3,31]{2,0,1:T(4,128)S(1)} %bitcast_divide_fusion), kind=kOutput, calls=%fused_computation.33 | convolution fusion | flops 30720256 | bytes 407552 | tf_op jit(solution)/shard_map/ijt,vt->vij/dot_general | solution.py:49
  50.2 0.9 %fusion.13 = f32[4,158,128,1]{2,0,1,3:T(4,128)S(1)} fusion(s32[158,128]{1,0:T(8,128)S(1)} %iota_subtract_fusion, f32[4,1,31]{2,0,1:T(4,128)S(1)} %slice.54), kind=kOutput, calls=%fused_computation.34 | convolution fusion | flops 30720256 | bytes 404976 | tf_op jit(solution)/shard_map/ijt,vt->vij/dot_general | solution.py:49
  52.1 0.5 convolution_bitcast_fusion.1
  52.6 0.7 convolution_bitcast_fusion.7
  53.6 0.9 fusion.8
  54.6 1.9 %collective-permute-start.2 = (bf16[4,8,32,15]{3,1,2,0:T(8,128)(2,1)S(1)}, bf16[4,8,32,15]{3,1,2,0:T(8,128)(2,1)S(1)}, u32[]{:S(2)}, u32[]{:S(2)}) collective-permute-start(bf16[4,8,32,15]{3,1,2,0:T(8,128)(2,1)S(1)} %get-tuple-element.7), channel_id=1, source_target_pairs={{0,1},{1,2},{2,3},{3,4},{4,5},{5,6},{6,7},{7,8},{8,9},{9,10},{10,1... | collective-permute-start | bytes 92168 | tf_op jit(solution)/shard_map/ppermute | solution.py:28
  56.5 2.4 %collective-permute-start.3 = (bf16[4,8,32,15]{3,1,2,0:T(8,128)(2,1)S(1)}, bf16[4,8,32,15]{3,1,2,0:T(8,128)(2,1)S(1)}, u32[]{:S(2)}, u32[]{:S(2)}) collective-permute-start(bf16[4,8,32,15]{3,1,2,0:T(8,128)(2,1)S(1)} %get-tuple-element.8), channel_id=1, source_target_pairs={{1,0},{2,1},{3,2},{4,3},{5,4},{6,5},{7,6},{8,7},{9,8},{10,9},{11,1... | collective-permute-start | bytes 92168 | tf_op jit(solution)/shard_map/ppermute | solution.py:30
  59.8 4.4 %collective-permute-done.3 = bf16[4,8,32,15]{3,1,2,0:T(8,128)(2,1)S(1)} collective-permute-done((bf16[4,8,32,15]{3,1,2,0:T(8,128)(2,1)S(1)}, bf16[4,8,32,15]{3,1,2,0:T(8,128)(2,1)S(1)}, u32[]{:S(2)}, u32[]{:S(2)}) %collective-permute-start.3) | collective-permute-done | bytes 30752 | tf_op jit(solution)/shard_map/ppermute | solution.py:30
  64.5 0.6 convolution_bitcast_fusion.6
  65.1 0.7 convolution_bitcast_fusion.5
  65.8 0.8 fusion.10
  66.9 1.9 %collective-permute-start.4 = (bf16[8,32,15]{2,1,0:T(8,128)(2,1)S(1)}, bf16[8,32,15]{2,1,0:T(8,128)(2,1)S(1)}, u32[]{:S(2)}, u32[]{:S(2)}) collective-permute-start(bf16[8,32,15]{2,1,0:T(8,128)(2,1)S(1)} %get-tuple-element.9), channel_id=1, source_target_pairs={{0,1},{1,2},{2,3},{3,4},{4,5},{5,6},{6,7},{7,8},{8,9},{9,10},{10,1... | collective-permute-start | bytes 23048 | tf_op jit(solution)/shard_map/ppermute | solution.py:28
  68.8 2.4 %collective-permute-start.5 = (bf16[8,32,15]{2,1,0:T(8,128)(2,1)S(1)}, bf16[8,32,15]{2,1,0:T(8,128)(2,1)S(1)}, u32[]{:S(2)}, u32[]{:S(2)}) collective-permute-start(bf16[8,32,15]{2,1,0:T(8,128)(2,1)S(1)} %get-tuple-element.10), channel_id=1, source_target_pairs={{1,0},{2,1},{3,2},{4,3},{5,4},{6,5},{7,6},{8,7},{9,8},{10,9},{11,1... | collective-permute-start | bytes 23048 | tf_op jit(solution)/shard_map/ppermute | solution.py:30
  71.2 3.2 %collective-permute-done.5 = bf16[8,32,15]{2,1,0:T(8,128)(2,1)S(1)} collective-permute-done((bf16[8,32,15]{2,1,0:T(8,128)(2,1)S(1)}, bf16[8,32,15]{2,1,0:T(8,128)(2,1)S(1)}, u32[]{:S(2)}, u32[]{:S(2)}) %collective-permute-start.5) | collective-permute-done | bytes 7712 | tf_op jit(solution)/shard_map/ppermute | solution.py:30
  74.4 0.5 convolution_bitcast_fusion
  74.8 0.7 convolution_bitcast_fusion.4
  75.6 0.9 fusion.9
  76.6 1.9 %collective-permute-start.6 = (bf16[4,8,32,15]{3,1,2,0:T(8,128)(2,1)S(1)}, bf16[4,8,32,15]{3,1,2,0:T(8,128)(2,1)S(1)}, u32[]{:S(2)}, u32[]{:S(2)}) collective-permute-start(bf16[4,8,32,15]{3,1,2,0:T(8,128)(2,1)S(1)} %get-tuple-element.5), channel_id=1, source_target_pairs={{0,1},{1,2},{2,3},{3,4},{4,5},{5,6},{6,7},{7,8},{8,9},{9,10},{10,1... | collective-permute-start | bytes 92168 | tf_op jit(solution)/shard_map/ppermute | solution.py:28
  78.5 2.6 %collective-permute-start.7 = (bf16[4,8,32,15]{3,1,2,0:T(8,128)(2,1)S(1)}, bf16[4,8,32,15]{3,1,2,0:T(8,128)(2,1)S(1)}, u32[]{:S(2)}, u32[]{:S(2)}) collective-permute-start(bf16[4,8,32,15]{3,1,2,0:T(8,128)(2,1)S(1)} %get-tuple-element.6), channel_id=1, source_target_pairs={{1,0},{2,1},{3,2},{4,3},{5,4},{6,5},{7,6},{8,7},{9,8},{10,9},{11,1... | collective-permute-start | bytes 92168 | tf_op jit(solution)/shard_map/ppermute | solution.py:30
  81.1 0.7 collective-permute-done.6
  81.8 4.6 %collective-permute-done.7 = bf16[4,8,32,15]{3,1,2,0:T(8,128)(2,1)S(1)} collective-permute-done((bf16[4,8,32,15]{3,1,2,0:T(8,128)(2,1)S(1)}, bf16[4,8,32,15]{3,1,2,0:T(8,128)(2,1)S(1)}, u32[]{:S(2)}, u32[]{:S(2)}) %collective-permute-start.7) | collective-permute-done | bytes 30752 | tf_op jit(solution)/shard_map/ppermute | solution.py:30
  86.7 0.6 convolution_bitcast_fusion.3
  87.3 0.7 convolution_bitcast_fusion.2
  88.0 0.8 fusion.11
  88.8 0.7 fusion.46
  (43 shorter events, 4.0 us)
Async XLA Ops:
  0.0 10.2 %copy-start.1 = (bf16[4,8,2,2048]{3,2,1,0:T(2,128)(2,1)S(1)}, bf16[4,8,2,2048]{3,2,1,0:T(2,128)(2,1)}, u32[]{:S(2)}) copy-start(bf16[4,8,2,2048]{3,2,1,0:T(2,128)(2,1)} %param.5) | copy-start | bytes 786436
  1.1 51.0 %collective-permute-start = (bf16[8,32,15]{2,1,0:T(8,128)(2,1)S(1)}, bf16[8,32,15]{2,1,0:T(8,128)(2,1)S(1)}, u32[]{:S(2)}, u32[]{:S(2)}) collective-permute-start(bf16[8,32,15]{2,1,0:T(8,128)(2,1)S(1)} %get-tuple-element.11), channel_id=1, source_target_pairs={{0,1},{1,2},{2,3},{3,4},{4,5},{5,6},{6,7},{7,8},{8,9},{9,10},{10,1... | collective-permute-start | bytes 23048 | tf_op jit(solution)/shard_map/ppermute | solution.py:28
  5.6 46.5 %collective-permute-start.1 = (bf16[8,32,15]{2,1,0:T(8,128)(2,1)S(1)}, bf16[8,32,15]{2,1,0:T(8,128)(2,1)S(1)}, u32[]{:S(2)}, u32[]{:S(2)}) collective-permute-start(bf16[8,32,15]{2,1,0:T(8,128)(2,1)S(1)} %get-tuple-element.12), channel_id=1, source_target_pairs={{1,0},{2,1},{3,2},{4,3},{5,4},{6,5},{7,6},{8,7},{9,8},{10,9},{11,1... | collective-permute-start | bytes 23048 | tf_op jit(solution)/shard_map/ppermute | solution.py:30
  11.4 13.9 %copy-start.4 = (s32[16]{0:T(128)S(1)}, s32[16]{0:T(128)}, u32[]{:S(2)}) copy-start(s32[16]{0:T(128)} %param.8) | copy-start | bytes 196
  11.4 14.5 %copy-start.2 = (f32[1,4,3,31]{3,1,2,0:T(4,128)S(1)}, f32[1,4,3,31]{3,1,2,0:T(4,128)}, u32[]{:S(2)}) copy-start(f32[1,4,3,31]{3,1,2,0:T(4,128)} %param.7) | copy-start | bytes 4468
  18.8 34.5 %all-to-all-start = ((bf16[16,4,8,2,128]{4,3,2,1,0:T(2,128)(2,1)}), bf16[16,4,8,2,128]{4,3,2,1,0:T(2,128)(2,1)S(1)}, u32[]{:S(2)}, u32[]{:S(2)}) async-start(bf16[16,4,8,2,128]{4,3,2,1,0:T(2,128)(2,1)} %constant_dynamic-update-slice_fusion), calls=%async_computation | async-start | bytes 524288 | tf_op jit(solution)/shard_map/all_to_all | solution.py:16
  25.2 24.7 %copy-start.3 = (s32[16,4]{0,1:T(4,128)S(1)}, s32[16,4]{0,1:T(4,128)}, u32[]{:S(2)}) copy-start(s32[16,4]{0,1:T(4,128)} %param.9) | copy-start | bytes 772
  54.6 5.2 %collective-permute-start.2 = (bf16[4,8,32,15]{3,1,2,0:T(8,128)(2,1)S(1)}, bf16[4,8,32,15]{3,1,2,0:T(8,128)(2,1)S(1)}, u32[]{:S(2)}, u32[]{:S(2)}) collective-permute-start(bf16[4,8,32,15]{3,1,2,0:T(8,128)(2,1)S(1)} %get-tuple-element.7), channel_id=1, source_target_pairs={{0,1},{1,2},{2,3},{3,4},{4,5},{5,6},{6,7},{7,8},{8,9},{9,10},{10,1... | collective-permute-start | bytes 92168 | tf_op jit(solution)/shard_map/ppermute | solution.py:28
  56.5 7.7 %collective-permute-start.3 = (bf16[4,8,32,15]{3,1,2,0:T(8,128)(2,1)S(1)}, bf16[4,8,32,15]{3,1,2,0:T(8,128)(2,1)S(1)}, u32[]{:S(2)}, u32[]{:S(2)}) collective-permute-start(bf16[4,8,32,15]{3,1,2,0:T(8,128)(2,1)S(1)} %get-tuple-element.8), channel_id=1, source_target_pairs={{1,0},{2,1},{3,2},{4,3},{5,4},{6,5},{7,6},{8,7},{9,8},{10,9},{11,1... | collective-permute-start | bytes 92168 | tf_op jit(solution)/shard_map/ppermute | solution.py:30
  65.8 0.9 %copy-start = (f32[8,32,128]{2,1,0:T(8,128)S(1)}, f32[8,32,128]{2,1,0:T(8,128)}, u32[]{:S(2)}) copy-start(f32[8,32,128]{2,1,0:T(8,128)} %param.6) | copy-start | bytes 393220
  66.9 4.3 %collective-permute-start.4 = (bf16[8,32,15]{2,1,0:T(8,128)(2,1)S(1)}, bf16[8,32,15]{2,1,0:T(8,128)(2,1)S(1)}, u32[]{:S(2)}, u32[]{:S(2)}) collective-permute-start(bf16[8,32,15]{2,1,0:T(8,128)(2,1)S(1)} %get-tuple-element.9), channel_id=1, source_target_pairs={{0,1},{1,2},{2,3},{3,4},{4,5},{5,6},{6,7},{7,8},{8,9},{9,10},{10,1... | collective-permute-start | bytes 23048 | tf_op jit(solution)/shard_map/ppermute | solution.py:28
  68.8 5.6 %collective-permute-start.5 = (bf16[8,32,15]{2,1,0:T(8,128)(2,1)S(1)}, bf16[8,32,15]{2,1,0:T(8,128)(2,1)S(1)}, u32[]{:S(2)}, u32[]{:S(2)}) collective-permute-start(bf16[8,32,15]{2,1,0:T(8,128)(2,1)S(1)} %get-tuple-element.10), channel_id=1, source_target_pairs={{1,0},{2,1},{3,2},{4,3},{5,4},{6,5},{7,6},{8,7},{9,8},{10,9},{11,1... | collective-permute-start | bytes 23048 | tf_op jit(solution)/shard_map/ppermute | solution.py:30
  76.6 5.2 %collective-permute-start.6 = (bf16[4,8,32,15]{3,1,2,0:T(8,128)(2,1)S(1)}, bf16[4,8,32,15]{3,1,2,0:T(8,128)(2,1)S(1)}, u32[]{:S(2)}, u32[]{:S(2)}) collective-permute-start(bf16[4,8,32,15]{3,1,2,0:T(8,128)(2,1)S(1)} %get-tuple-element.5), channel_id=1, source_target_pairs={{0,1},{1,2},{2,3},{3,4},{4,5},{5,6},{6,7},{7,8},{8,9},{9,10},{10,1... | collective-permute-start | bytes 92168 | tf_op jit(solution)/shard_map/ppermute | solution.py:28
  78.5 7.8 %collective-permute-start.7 = (bf16[4,8,32,15]{3,1,2,0:T(8,128)(2,1)S(1)}, bf16[4,8,32,15]{3,1,2,0:T(8,128)(2,1)S(1)}, u32[]{:S(2)}, u32[]{:S(2)}) collective-permute-start(bf16[4,8,32,15]{3,1,2,0:T(8,128)(2,1)S(1)} %get-tuple-element.6), channel_id=1, source_target_pairs={{1,0},{2,1},{3,2},{4,3},{5,4},{6,5},{7,6},{8,7},{9,8},{10,9},{11,1... | collective-permute-start | bytes 92168 | tf_op jit(solution)/shard_map/ppermute | solution.py:30
